TPU v7x, 32 devices: a whole 2x2x4 slice. The times are simulated.
32 devices in a mesh: groups: 2 (over y), ctx: 4 (over z), head: 2 (over x), feat: 2 (over core).
Axes of the slice: x: 2, y: 2, z: 4, core: 2. Of those that a mesh axis runs over, the one named last changes fastest.
Arguments:
- queries: bfloat16 [1024, 5120], P(('groups', 'ctx'), 'head'), parts along dimension 0, may hold values from -6 to 6
- keys: bfloat16 [1024, 1024], P(('groups', 'ctx'), 'head'), parts along dimension 0, may hold values from -6 to 6
- values: bfloat16 [1024, 1024], P(('groups', 'ctx'), 'head'), parts along dimension 0, may hold values from -6 to 6
- log_gate: float32 [1024, 8], P(('groups', 'ctx'), 'head'), parts along dimension 0, may hold values from -1 to 0, as said below
- cand_q: bfloat16 [128, 5120], P('groups', 'head'), parts along dimension 0, may hold values from -12 to 12
- cand_kv: bfloat16 [128, 2, 1024], P('groups', None, 'head'), parts along dimension 0, may hold values from -12 to 12
- token_ids: int32 [32], P('groups'), parts along dimension 0, may hold values from 0 to 63
- fork_pos: int32 [32], P('groups'), parts along dimension 0, may hold values from 1 to 4
- slot_map: int32 [32], P('groups'), parts along dimension 0, may hold values from 0 to 15, each once
Outputs:
- prefill_out: bfloat16 [1024, 5120], P(('groups', 'ctx', 'feat'), 'head'), parts along dimension 0
- branch_out: bfloat16 [32, 5120], P(('groups', 'ctx', 'feat'), 'head'), parts along dimension 0
There are 2 independent parts, one for each index of `groups`. A program takes and returns all parts, laid end to end along the dimension named above; each array names one. Nothing has to cross between parts.
Inputs may be any that keep to these rules, and one draw needn't show every extreme that they name: log_gate is never positive.
All inputs are finite; a program needn't handle non-finite values.
Results may differ from a plain program's by a relative error of at most 0.0055.
Values may be sent and summed in bfloat16 or wider, within the bound.
A program may use at most 192 MiB of HBM per device.

v0:
```python
import math

import jax
import jax.numpy as jnp
from jax import lax
from jax.sharding import PartitionSpec as P

HEAD = 128
GROUP = 5


def carried_in(shard, axis, combine, identity):
    count, mine = (lax.axis_size(axis), lax.axis_index(axis))
    everything = jax.tree.map(lambda part: lax.all_gather(part, axis), shard)
    start = jax.tree.map(
        lambda part, zero: jnp.broadcast_to(jnp.asarray(zero, part.dtype), part.shape),
        shard,
        identity,
    )

    def step(k, before):
        reached = k < mine
        new = combine(before, jax.tree.map(lambda part: part[k], everything))
        return jax.tree.map(lambda a, b: jnp.where(reached, a, b), new, before)

    return lax.fori_loop(0, count, step, start)


def expand_part(block, parity):
    wide = block.astype(jnp.float32)
    rows = wide.shape[0]
    width = wide.shape[1]
    quarter = width // 4
    doubled = jnp.concatenate([wide, wide], axis=1)
    shifted = lax.dynamic_slice_in_dim(doubled, parity, 2 * width - 1, 1)
    partner = jnp.stack(
        [shifted[:, 2 * step : 2 * step + width] for step in range(quarter)], axis=1
    )
    offsets = parity + 2 * lax.broadcasted_iota(jnp.int32, (quarter,), 0)
    weight = jnp.where(offsets == 0, 1.0, math.sqrt(2.0)).astype(jnp.float32)
    bulk = (wide[:, None, :] * partner * weight[None, :, None]).reshape(rows, quarter * width)
    lower = lax.dynamic_slice_in_dim(wide, parity * quarter, quarter, 1)
    upper = lax.dynamic_slice_in_dim(wide, parity * quarter + width // 2, quarter, 1)
    tail = lower * upper * math.sqrt(2.0)
    return jnp.concatenate([bulk, tail], axis=1).astype(jnp.bfloat16)


def chain_combine(earlier, later):
    decay = earlier[0] * later[0]
    states = later[0][:, None, None] * earlier[1] + later[1]
    norms = later[0][:, None] * earlier[2] + later[2]
    return (decay, states, norms)


def per_device(queries, keys, values, log_gate, cand_q, cand_kv, token_ids, fork_pos, slot_map):
    feat_count = lax.axis_size("feat")
    feat_index = lax.axis_index("feat")
    ctx_index = lax.axis_index("ctx")
    length = queries.shape[0]
    kv_local = keys.shape[1] // HEAD
    cumul = jnp.cumsum(log_gate, axis=0)
    finals = cumul[-1]
    carry_w = jnp.exp(finals[None, :] - cumul)
    state_list = []
    norm_list = []
    for head in range(kv_local):
        key_h = keys[:, head * HEAD : (head + 1) * HEAD]
        value_h = values[:, head * HEAD : (head + 1) * HEAD]
        phik = expand_part(key_h, feat_index)
        scaled = (carry_w[:, head : head + 1] * value_h.astype(jnp.float32)).astype(jnp.bfloat16)
        state_list.append(
            lax.dot_general(
                phik, scaled, (((0,), (0,)), ((), ())), preferred_element_type=jnp.float32
            )
        )
        norm_list.append(
            jnp.dot(carry_w[:, head].astype(jnp.bfloat16), phik, preferred_element_type=jnp.float32)
        )
    local_states = jnp.stack(state_list)
    local_norms = jnp.stack(norm_list)
    decays = jnp.exp(finals)
    identity = (jnp.ones_like(decays), jnp.zeros_like(local_states), jnp.zeros_like(local_norms))
    scanned = carried_in((decays, local_states, local_norms), "ctx", chain_combine, identity)
    prior_states = scanned[1]
    prior_norms = scanned[2]
    prior_sb = prior_states.astype(jnp.bfloat16)
    prior_zb = prior_norms.astype(jnp.bfloat16)
    part_rows = length // feat_count
    row_start = feat_index * part_rows
    own_q = lax.dynamic_slice_in_dim(queries, row_start, part_rows, 0)
    own_cum = lax.dynamic_slice_in_dim(cumul, row_start, part_rows, 0)
    inter_num = []
    inter_den = []
    for head in range(kv_local):
        growth = jnp.exp(cumul[:, head])
        for member in range(GROUP):
            column = (head * GROUP + member) * HEAD
            phiq = expand_part(queries[:, column : column + HEAD], feat_index)
            inter_num.append(
                jnp.dot(phiq, prior_sb[head], preferred_element_type=jnp.float32)
                * growth[:, None]
                / HEAD
            )
            inter_den.append(
                jnp.dot(phiq, prior_zb[head], preferred_element_type=jnp.float32) * growth / HEAD
            )
    summed_num, summed_den = (
        lax.psum_scatter(
            jnp.concatenate(inter_num, axis=1), "feat", scatter_dimension=0, tiled=True
        ),
        lax.psum_scatter(jnp.stack(inter_den, axis=1), "feat", scatter_dimension=0, tiled=True),
    )
    row_pos = row_start + lax.broadcasted_iota(jnp.int32, (part_rows, length), 0)
    col_pos = lax.broadcasted_iota(jnp.int32, (part_rows, length), 1)
    causal = col_pos <= row_pos
    prefill_pieces = []
    for head in range(kv_local):
        key_h = keys[:, head * HEAD : (head + 1) * HEAD]
        value_h = values[:, head * HEAD : (head + 1) * HEAD]
        spread = own_cum[:, head][:, None] - cumul[:, head][None, :]
        fading = jnp.where(causal, jnp.exp(jnp.where(causal, spread, 0.0)), 0.0)
        for member in range(GROUP):
            index = head * GROUP + member
            raw = lax.dot_general(
                own_q[:, index * HEAD : (index + 1) * HEAD],
                key_h,
                (((1,), (1,)), ((), ())),
                preferred_element_type=jnp.float32,
            )
            weights = raw * raw / HEAD * fading
            numer = summed_num[:, index * HEAD : (index + 1) * HEAD] + jnp.dot(
                weights.astype(jnp.bfloat16), value_h, preferred_element_type=jnp.float32
            )
            denom = summed_den[:, index] + jnp.sum(weights, axis=1)
            prefill_pieces.append((numer / jnp.maximum(denom, 1.0)[:, None]).astype(jnp.bfloat16))
    prefill_out = jnp.concatenate(prefill_pieces, axis=1)
    branches = token_ids.shape[0]
    order = (slot_map[None, :] == lax.broadcasted_iota(jnp.int32, (branches, branches), 0)).astype(
        jnp.int32
    )
    ids_sorted = jnp.sum(order * token_ids[None, :], axis=1)
    fork_sorted = jnp.sum(order * fork_pos[None, :], axis=1)
    pick = (
        ids_sorted[:, None] == lax.broadcasted_iota(jnp.int32, (branches, cand_q.shape[0]), 1)
    ).astype(jnp.bfloat16)
    new_q = jnp.dot(pick, cand_q, preferred_element_type=jnp.float32).astype(jnp.bfloat16)
    new_kv = jnp.einsum("bc,cpd->bpd", pick, cand_kv, preferred_element_type=jnp.float32).astype(
        jnp.bfloat16
    )
    included_states = decays[:, None, None] * prior_states + local_states
    included_norms = decays[:, None] * prior_norms + local_norms
    dnum_list = []
    dden_list = []
    chosen = (fork_sorted - 1 == ctx_index).astype(jnp.float32)
    for head in range(kv_local):
        state_b = included_states[head].astype(jnp.bfloat16)
        norm_b = included_norms[head].astype(jnp.bfloat16)
        for member in range(GROUP):
            column = (head * GROUP + member) * HEAD
            phiq = expand_part(new_q[:, column : column + HEAD], feat_index)
            dnum_list.append(
                jnp.dot(phiq, state_b, preferred_element_type=jnp.float32) * chosen[:, None] / HEAD
            )
            dden_list.append(
                jnp.dot(phiq, norm_b, preferred_element_type=jnp.float32) * chosen / HEAD
            )
    total_num, total_den = (
        lax.psum_scatter(
            jnp.concatenate(dnum_list, axis=1), ("ctx", "feat"), scatter_dimension=0, tiled=True
        ),
        lax.psum_scatter(
            jnp.stack(dden_list, axis=1), ("ctx", "feat"), scatter_dimension=0, tiled=True
        ),
    )
    owned = total_num.shape[0]
    first = (ctx_index * feat_count + feat_index) * owned
    mine_q = lax.dynamic_slice_in_dim(new_q, first, owned, 0)
    mine_kv = lax.dynamic_slice_in_dim(new_kv, first, owned, 0)
    branch_pieces = []
    for head in range(kv_local):
        key_n = mine_kv[:, 0, head * HEAD : (head + 1) * HEAD].astype(jnp.float32)
        value_n = mine_kv[:, 1, head * HEAD : (head + 1) * HEAD].astype(jnp.float32)
        for member in range(GROUP):
            index = head * GROUP + member
            query_n = mine_q[:, index * HEAD : (index + 1) * HEAD].astype(jnp.float32)
            inner = jnp.sum(query_n * key_n, axis=1)
            own_weight = inner * inner / HEAD
            numer = total_num[:, index * HEAD : (index + 1) * HEAD] + own_weight[:, None] * value_n
            denom = total_den[:, index] + own_weight
            branch_pieces.append((numer / jnp.maximum(denom, 1.0)[:, None]).astype(jnp.bfloat16))
    branch_out = jnp.concatenate(branch_pieces, axis=1)
    return (prefill_out, branch_out)


def solution(mesh):
    return jax.shard_map(
        per_device,
        mesh=mesh,
        in_specs=(
            P(("groups", "ctx"), "head"),
            P(("groups", "ctx"), "head"),
            P(("groups", "ctx"), "head"),
            P(("groups", "ctx"), "head"),
            P("groups", "head"),
            P("groups", None, "head"),
            P("groups"),
            P("groups"),
            P("groups"),
        ),
        out_specs=(P(("groups", "ctx", "feat"), "head"), P(("groups", "ctx", "feat"), "head")),
        check_vma=False,
    )
```

profile of v0, /device:TPU:1, one launch (start us, length us, event | category | flops | bytes accessed | tf_op | source)
XLA Modules:
  0.0 847.1 jit_solution(6095518286896023935)
XLA Ops:
  7.2 1.8 fusion.797
  17.5 1.6 broadcast_multiply_fusion.14
  41.8 1.6 broadcast_multiply_fusion.20
  49.0 21.1 %fusion.3 = (bf16[128,4096]{0,1:T(8,128)(2,1)}, bf16[128,4096]{0,1:T(8,128)(2,1)}, bf16[128,4096]{0,1:T(8,128)(2,1)}, bf16[128,4096]{0,1:T(8,128)(2,1)}, bf16[12...) fusion(f32[128,32,128]{0,2,1:T(8,128)} %broadcast_multiply_fusi, ...), kind=kLoop, calls=%fused_computation.1502 | loop fusion | flops 18874368 | bytes 56639488 | tf_op jit(solution)/shard_map/convert.56
  70.0 1.8 convolution_bitcast_fusion.1
  76.2 3.5 pad_maximum_fusion
  79.8 2.4 fusion.267
  82.2 2.3 fusion.268
  110.6 45.9 %all-gather.3 = f32[4,4,4128]{2,1,0:T(4,128)S(1)} all-gather(f32[1,4,4128]{2,1,0:T(4,128)S(1)} %fusion.453), channel_id=3, replica_groups=mesh['groups'=2,'ctx'=4,'head'=2,'feat'=2] {'ctx'}, dimensions={0}, use_global_device_ids=true | all-gather | bytes 330240 | tf_op jit(solution)/shard_map/all_gather | solution.py:14
  156.5 7.4 all-gather.2
  213.2 2.2 fusion.800
  215.4 2.2 fusion.801
  217.6 2.1 fusion.802
  219.7 2.1 fusion.803
  221.8 2.2 fusion.804
  224.0 2.2 fusion.805
  226.2 2.2 fusion.806
  228.3 2.2 fusion.807
  230.6 2.1 fusion.808
  232.7 2.2 fusion.809
  234.9 2.2 fusion.810
  237.1 2.1 fusion.811
  239.2 1.6 fusion.550
  241.4 2.2 fusion.812
  243.6 1.6 fusion.568
  258.5 2.2 fusion.813
  260.7 2.2 fusion.814
  262.9 2.2 fusion.815
  265.0 2.1 fusion.816
  267.1 2.2 fusion.817
  269.3 2.2 fusion.818
  271.5 2.2 fusion.819
  276.7 9.8 %constant_dynamic-update-slice_fusion.717 = f32[128,32,128]{0,2,1:T(8,128)S(1)} fusion(f32[128,32,128]{0,2,1:T(8,128)S(1)} %constant_dynamic-update-slice_fusion.718, f32[128,255]{0,1:T(8,128)S(1)} %get-tuple-element.430), kind=kLoop, calls=%fused_computation.730 | loop fusion | bytes 131072
  290.8 1.6 fusion.271
  292.4 4.1 fusion.4
  296.5 357.2 %all-gather.6.cloned.1.call-done = f32[16,4128,128]{2,1,0:T(8,128)} async-done(((f32[4,4128,128]{2,1,0:T(8,128)}), f32[16,4128,128]{2,1,0:T(8,128)}) %all-gather.6.cloned.1.call-update) | async-done | bytes 33816592 | tf_op jit(solution)/shard_map/all_gather | solution.py:14
  653.7 42.2 %while.16 = (s32[]{:T(128)}, f32[4,4128,128]{2,1,0:T(8,128)}, f32[4,4128]{1,0:T(4,128)S(1)}, s32[]{:T(128)}, f32[4,4]{1,0:T(4,128)}, /*index=5*/f32[4,4,4128,128...) while((s32[]{:T(128)}, f32[4,4128,128]{2,1,0:T(8,128)}, f32[4,4128]{1,0:T(4,128)S(1)}, ...), condition=%wide.region_2.3_spmd.clone, body=%wide.region_1.2_spmd.clone.sunk | while | flops 8520196 | bytes 25560768 | solution.py:26
  654.5 7.8 fusion.845
  663.1 10.3 %fusion.845 = f32[4,4128,128]{2,1,0:T(8,128)} fusion(f32[4,4,4128,128]{3,2,1,0:T(8,128)} %get-tuple-element.597, s32[]{:T(128)} %get-tuple-element.583, f32[4,4128,128]{2,1,0:T(8,128)} %get-tuple-element.584, f32[4]{0:T(128)S(1)} %fusion.844, pred[]{:T(512)S(6)} %compare.3, pred[]{:T(512)S(6)} %lt.38), kind=kLoop, calls=%fused_computation.1.clone.1 | loop fusion | flops 8454144 | bytes 25362454 | tf_op jit(solution)/shard_map/while/body/eval_jaxpr/jit(_where)/select_n | solution.py:24
  674.2 10.3 %fusion.845 = f32[4,4128,128]{2,1,0:T(8,128)} fusion(f32[4,4,4128,128]{3,2,1,0:T(8,128)} %get-tuple-element.597, s32[]{:T(128)} %get-tuple-element.583, f32[4,4128,128]{2,1,0:T(8,128)} %get-tuple-element.584, f32[4]{0:T(128)S(1)} %fusion.844, pred[]{:T(512)S(6)} %compare.3, pred[]{:T(512)S(6)} %lt.38), kind=kLoop, calls=%fused_computation.1.clone.1 | loop fusion | flops 8454144 | bytes 25362454 | tf_op jit(solution)/shard_map/while/body/eval_jaxpr/jit(_where)/select_n | solution.py:24
  685.3 10.5 %fusion.845 = f32[4,4128,128]{2,1,0:T(8,128)} fusion(f32[4,4,4128,128]{3,2,1,0:T(8,128)} %get-tuple-element.597, s32[]{:T(128)} %get-tuple-element.583, f32[4,4128,128]{2,1,0:T(8,128)} %get-tuple-element.584, f32[4]{0:T(128)S(1)} %fusion.844, pred[]{:T(512)S(6)} %compare.3, pred[]{:T(512)S(6)} %lt.38), kind=kLoop, calls=%fused_computation.1.clone.1 | loop fusion | flops 8454144 | bytes 25362454 | tf_op jit(solution)/shard_map/while/body/eval_jaxpr/jit(_where)/select_n | solution.py:24
  696.1 10.6 %add_convert_fusion = (bf16[4,4128,128]{2,1,0:T(8,128)(2,1)S(1)}, bf16[4,4128,128]{2,1,0:T(8,128)(2,1)}) fusion(f32[4,4128,128]{2,1,0:T(8,128)} %get-tuple-element.127, f32[4]{0:T(128)S(1)} %copy-done.227, f32[1,4128,128]{2,1,0:T(8,128)} %copy-done.4, f32[1,4128,128]{2,1,0:T(8,128)S(1)} %convolution_bitcast_fusion.1, f32[1,4128,128]{2,1,0:T(8,128)} %copy-done.2, ...), kind=kLoop, calls=%fused_computation.7 | loop fusion | flops 14794752 | bytes 25362448 | tf_op jit(solution)/shard_map/convert.53
  728.3 2.2 constant_dynamic-update-slice_fusion.787
  730.5 2.1 constant_dynamic-update-slice_fusion.786
  732.7 1.9 constant_dynamic-update-slice_fusion.785
  754.5 23.4 %all-reduce.1 = f32[16,20]{0,1:T(8,128)S(1)} all-reduce(f32[16,20]{0,1:T(8,128)S(1)} %stack.6015), channel_id=7, replica_groups=mesh['groups'=2,'ctx'=4,'head'=2,'feat'=2] {'ctx','feat'}, use_global_device_ids=true, to_apply=%region_29.30.clone | all-reduce | flops 320 | bytes 2560
  778.6 2.2 fusion.799
  796.1 9.4 %all-reduce.4.cloned.1.call-done = f32[16,2560]{1,0:T(8,128)} async-done(((f32[16,2560]{1,0:T(8,128)}), f32[16,2560]{1,0:T(8,128)}) %all-reduce.4.cloned.1.call-update) | async-done | bytes 163856
  (2327 shorter events, 222.5 us)
Async XLA Ops:
  7.2 80.5 %copy-start = (bf16[64,2560]{1,0:T(8,128)(2,1)S(1)}, bf16[64,2560]{1,0:T(8,128)(2,1)}, u32[]{:S(2)}) copy-start(bf16[64,2560]{1,0:T(8,128)(2,1)} %param.15) | copy-start | bytes 983044
  7.2 646.6 %all-gather.6.cloned.1.call-start = ((), (), s32[]{:S(2)}) async-start(), calls=%async_computation.2 | async-start | bytes 42270720 | tf_op jit(solution)/shard_map/all_gather | solution.py:14
  79.8 698.8 %reduce-scatter.10.cloned.1.call-start = ((), (), s32[]{:S(2)}) async-start(), calls=%async_computation.4 | async-start | bytes 98304
  653.7 42.2 %copy-start.158 = (f32[1,4128]{1,0:T(1,128)S(1)}, f32[1,4128]{1,0:T(1,128)}, u32[]{:S(2)}) copy-start(f32[1,4128]{1,0:T(1,128)} %fusion.268) | copy-start | bytes 49540
  653.7 42.2 %copy-start.159 = (f32[1,4128]{1,0:T(1,128)S(1)}, f32[1,4128]{1,0:T(1,128)}, u32[]{:S(2)}) copy-start(f32[1,4128]{1,0:T(1,128)} %fusion.269) | copy-start | bytes 49540
  653.7 42.2 %copy-start.160 = (f32[1,4128]{1,0:T(1,128)S(1)}, f32[1,4128]{1,0:T(1,128)}, u32[]{:S(2)}) copy-start(f32[1,4128]{1,0:T(1,128)} %fusion.270) | copy-start | bytes 49540
  653.7 42.2 %copy-start.227 = (f32[4]{0:T(128)S(1)}, f32[4]{0:T(128)}, u32[]{:S(2)}) copy-start(f32[4]{0:T(128)} %fusion.775) | copy-start | bytes 52
  728.0 77.5 %all-reduce.4.cloned.1.call-start = ((), (), s32[]{:S(2)}) async-start(), calls=%async_computation.5 | async-start | bytes 327680
  754.0 51.5 %copy-start.232 = (f32[2]{0:T(128)S(1)}, f32[2]{0:T(128)}, u32[]{:S(2)}) copy-start(f32[2]{0:T(128)} %get-tuple-element.480) | copy-start | bytes 28
  754.0 53.1 %copy-start.251 = (f32[2]{0:T(128)S(1)}, f32[2]{0:T(128)}, u32[]{:S(2)}) copy-start(f32[2]{0:T(128)} %get-tuple-element.490) | copy-start | bytes 28
  754.0 53.9 %copy-start.250 = (f32[2]{0:T(128)S(1)}, f32[2]{0:T(128)}, u32[]{:S(2)}) copy-start(f32[2]{0:T(128)} %get-tuple-element.489) | copy-start | bytes 28
  754.0 54.6 %copy-start.249 = (f32[2]{0:T(128)S(1)}, f32[2]{0:T(128)}, u32[]{:S(2)}) copy-start(f32[2]{0:T(128)} %get-tuple-element.488) | copy-start | bytes 28
  754.0 55.4 %copy-start.248 = (f32[2]{0:T(128)S(1)}, f32[2]{0:T(128)}, u32[]{:S(2)}) copy-start(f32[2]{0:T(128)} %get-tuple-element.487) | copy-start | bytes 28
  754.1 56.2 %copy-start.247 = (f32[2]{0:T(128)S(1)}, f32[2]{0:T(128)}, u32[]{:S(2)}) copy-start(f32[2]{0:T(128)} %get-tuple-element.486) | copy-start | bytes 28
  754.1 57.0 %copy-start.246 = (f32[2]{0:T(128)S(1)}, f32[2]{0:T(128)}, u32[]{:S(2)}) copy-start(f32[2]{0:T(128)} %get-tuple-element.485) | copy-start | bytes 28
  754.1 57.7 %copy-start.245 = (f32[2]{0:T(128)S(1)}, f32[2]{0:T(128)}, u32[]{:S(2)}) copy-start(f32[2]{0:T(128)} %get-tuple-element.484) | copy-start | bytes 28
  754.1 58.5 %copy-start.244 = (f32[2]{0:T(128)S(1)}, f32[2]{0:T(128)}, u32[]{:S(2)}) copy-start(f32[2]{0:T(128)} %get-tuple-element.483) | copy-start | bytes 28
  754.1 59.3 %copy-start.243 = (f32[2]{0:T(128)S(1)}, f32[2]{0:T(128)}, u32[]{:S(2)}) copy-start(f32[2]{0:T(128)} %get-tuple-element.482) | copy-start | bytes 28
  754.1 60.1 %copy-start.242 = (f32[2]{0:T(128)S(1)}, f32[2]{0:T(128)}, u32[]{:S(2)}) copy-start(f32[2]{0:T(128)} %get-tuple-element.481) | copy-start | bytes 28
  754.1 60.8 %copy-start.237 = (f32[2]{0:T(128)S(1)}, f32[2]{0:T(128)}, u32[]{:S(2)}) copy-start(f32[2]{0:T(128)} %get-tuple-element.479) | copy-start | bytes 28
  754.1 61.6 %copy-start.241 = (f32[2]{0:T(128)S(1)}, f32[2]{0:T(128)}, u32[]{:S(2)}) copy-start(f32[2]{0:T(128)} %get-tuple-element.478) | copy-start | bytes 28
  754.1 62.4 %copy-start.240 = (f32[2]{0:T(128)S(1)}, f32[2]{0:T(128)}, u32[]{:S(2)}) copy-start(f32[2]{0:T(128)} %get-tuple-element.477) | copy-start | bytes 28
  754.1 63.2 %copy-start.239 = (f32[2]{0:T(128)S(1)}, f32[2]{0:T(128)}, u32[]{:S(2)}) copy-start(f32[2]{0:T(128)} %get-tuple-element.476) | copy-start | bytes 28
  754.2 63.9 %copy-start.238 = (f32[2]{0:T(128)S(1)}, f32[2]{0:T(128)}, u32[]{:S(2)}) copy-start(f32[2]{0:T(128)} %get-tuple-element.475) | copy-start | bytes 28
  754.2 64.7 %copy-start.236 = (f32[2]{0:T(128)S(1)}, f32[2]{0:T(128)}, u32[]{:S(2)}) copy-start(f32[2]{0:T(128)} %get-tuple-element.474) | copy-start | bytes 28
  754.2 65.5 %copy-start.235 = (f32[2]{0:T(128)S(1)}, f32[2]{0:T(128)}, u32[]{:S(2)}) copy-start(f32[2]{0:T(128)} %get-tuple-element.473) | copy-start | bytes 28
  754.2 67.0 %copy-start.136 = (bf16[128,512]{1,0:T(8,128)(2,1)S(1)}, bf16[128,512]{1,0:T(8,128)(2,1)}, u32[]{:S(2)}) copy-start(bf16[128,512]{1,0:T(8,128)(2,1)} %param.13) | copy-start | bytes 393220
  754.2 67.0 %reduce-scatter.8.cloned.1.call-start = ((), (), s32[]{:S(2)}) async-start(), calls=%async_computation.3 | async-start | bytes 1966080 | tf_op jit(solution)/shard_map/reduce_scatter | solution.py:108
  778.4 51.9 %copy-start.270 = (bf16[64,128]{1,0:T(8,128)(2,1)S(1)}, bf16[64,128]{1,0:T(8,128)(2,1)}, u32[]{:S(2)}) copy-start(bf16[64,128]{1,0:T(8,128)(2,1)} %get-tuple-element.366) | copy-start | bytes 49156
  778.5 44.6 %copy-start.278 = (bf16[64,128]{1,0:T(8,128)(2,1)S(1)}, bf16[64,128]{1,0:T(8,128)(2,1)}, u32[]{:S(2)}) copy-start(bf16[64,128]{1,0:T(8,128)(2,1)} %get-tuple-element.350) | copy-start | bytes 49156
  778.5 45.5 %copy-start.277 = (bf16[64,128]{1,0:T(8,128)(2,1)S(1)}, bf16[64,128]{1,0:T(8,128)(2,1)}, u32[]{:S(2)}) copy-start(bf16[64,128]{1,0:T(8,128)(2,1)} %get-tuple-element.352) | copy-start | bytes 49156
  778.5 46.4 %copy-start.276 = (bf16[64,128]{1,0:T(8,128)(2,1)S(1)}, bf16[64,128]{1,0:T(8,128)(2,1)}, u32[]{:S(2)}) copy-start(bf16[64,128]{1,0:T(8,128)(2,1)} %get-tuple-element.354) | copy-start | bytes 49156
  778.5 47.3 %copy-start.275 = (bf16[64,128]{1,0:T(8,128)(2,1)S(1)}, bf16[64,128]{1,0:T(8,128)(2,1)}, u32[]{:S(2)}) copy-start(bf16[64,128]{1,0:T(8,128)(2,1)} %get-tuple-element.356) | copy-start | bytes 49156
  778.5 48.2 %copy-start.274 = (bf16[64,128]{1,0:T(8,128)(2,1)S(1)}, bf16[64,128]{1,0:T(8,128)(2,1)}, u32[]{:S(2)}) copy-start(bf16[64,128]{1,0:T(8,128)(2,1)} %get-tuple-element.358) | copy-start | bytes 49156
  778.5 49.1 %copy-start.273 = (bf16[64,128]{1,0:T(8,128)(2,1)S(1)}, bf16[64,128]{1,0:T(8,128)(2,1)}, u32[]{:S(2)}) copy-start(bf16[64,128]{1,0:T(8,128)(2,1)} %get-tuple-element.360) | copy-start | bytes 49156
  778.5 50.0 %copy-start.272 = (bf16[64,128]{1,0:T(8,128)(2,1)S(1)}, bf16[64,128]{1,0:T(8,128)(2,1)}, u32[]{:S(2)}) copy-start(bf16[64,128]{1,0:T(8,128)(2,1)} %get-tuple-element.362) | copy-start | bytes 49156
  778.5 50.9 %copy-start.271 = (bf16[64,128]{1,0:T(8,128)(2,1)S(1)}, bf16[64,128]{1,0:T(8,128)(2,1)}, u32[]{:S(2)}) copy-start(bf16[64,128]{1,0:T(8,128)(2,1)} %get-tuple-element.364) | copy-start | bytes 49156
  778.5 52.7 %copy-start.269 = (bf16[64,128]{1,0:T(8,128)(2,1)S(1)}, bf16[64,128]{1,0:T(8,128)(2,1)}, u32[]{:S(2)}) copy-start(bf16[64,128]{1,0:T(8,128)(2,1)} %get-tuple-element.368) | copy-start | bytes 49156
  778.6 43.6 %copy-start.279 = (bf16[64,128]{1,0:T(8,128)(2,1)S(1)}, bf16[64,128]{1,0:T(8,128)(2,1)}, u32[]{:S(2)}) copy-start(bf16[64,128]{1,0:T(8,128)(2,1)} %get-tuple-element.348) | copy-start | bytes 49156
  778.6 53.5 %copy-start.280 = (bf16[64,128]{1,0:T(8,128)(2,1)S(1)}, bf16[64,128]{1,0:T(8,128)(2,1)}, u32[]{:S(2)}) copy-start(bf16[64,128]{1,0:T(8,128)(2,1)} %get-tuple-element.370) | copy-start | bytes 49156
  778.6 54.4 %copy-start.286 = (bf16[64,128]{1,0:T(8,128)(2,1)S(1)}, bf16[64,128]{1,0:T(8,128)(2,1)}, u32[]{:S(2)}) copy-start(bf16[64,128]{1,0:T(8,128)(2,1)} %get-tuple-element.372) | copy-start | bytes 49156
  780.8 53.1 %copy-start.284 = (bf16[64,128]{1,0:T(8,128)(2,1)S(1)}, bf16[64,128]{1,0:T(8,128)(2,1)}, u32[]{:S(2)}) copy-start(bf16[64,128]{1,0:T(8,128)(2,1)} %get-tuple-element.374) | copy-start | bytes 49156
  780.9 54.0 %copy-start.287 = (bf16[64,128]{1,0:T(8,128)(2,1)S(1)}, bf16[64,128]{1,0:T(8,128)(2,1)}, u32[]{:S(2)}) copy-start(bf16[64,128]{1,0:T(8,128)(2,1)} %get-tuple-element.376) | copy-start | bytes 49156
  780.9 54.9 %copy-start.285 = (bf16[64,128]{1,0:T(8,128)(2,1)S(1)}, bf16[64,128]{1,0:T(8,128)(2,1)}, u32[]{:S(2)}) copy-start(bf16[64,128]{1,0:T(8,128)(2,1)} %get-tuple-element.378) | copy-start | bytes 49156
  781.8 54.8 %copy-start.283 = (bf16[64,128]{1,0:T(8,128)(2,1)S(1)}, bf16[64,128]{1,0:T(8,128)(2,1)}, u32[]{:S(2)}) copy-start(bf16[64,128]{1,0:T(8,128)(2,1)} %get-tuple-element.380) | copy-start | bytes 49156
  782.2 55.3 %copy-start.282 = (bf16[64,128]{1,0:T(8,128)(2,1)S(1)}, bf16[64,128]{1,0:T(8,128)(2,1)}, u32[]{:S(2)}) copy-start(bf16[64,128]{1,0:T(8,128)(2,1)} %get-tuple-element.382) | copy-start | bytes 49156
  782.6 55.8 %copy-start.281 = (bf16[64,128]{1,0:T(8,128)(2,1)S(1)}, bf16[64,128]{1,0:T(8,128)(2,1)}, u32[]{:S(2)}) copy-start(bf16[64,128]{1,0:T(8,128)(2,1)} %get-tuple-element.384) | copy-start | bytes 49156
  783.1 57.0 %copy-start.1 = (bf16[64,2560]{1,0:T(8,128)(2,1)S(1)}, bf16[64,2560]{1,0:T(8,128)(2,1)}, u32[]{:S(2)}) copy-start(bf16[64,2560]{1,0:T(8,128)(2,1)} %param.15) | copy-start | bytes 983044
  (247 other events, 1785.7 us)
Sparse Core Ops, SparseCore 0:
  79.9 573.7 all-gather.5
  728.1 6.7 reduce-scatter.9
  754.3 51.1 all-reduce.3
  807.8 10.5 reduce-scatter.7
where the time goes:
time: 862 us; the launch traced here: 847 us
  waiting for transfers between devices  367 us (43%)
  other arithmetic  171 us (20%)
  local copies, waits for them, and re-layouts  105 us (12%)
  matrix products  102 us (12%)
  blocking collectives  76.8 us (9%)
  between operations  25 us (3%)
    all_gather x1, waiting for transfers between devices, carried_in(): everything = jax.tree.map(lambda part: lax.all_gather(part, axis), shard)  357 us
    unnamed x1993, local copies, waits for them, and re-layouts  93.3 us
    another operation x28, other arithmetic  55.8 us
    all_gather x2, blocking collectives, carried_in(): everything = jax.tree.map(lambda part: lax.all_gather(part, axis), shard)  53.3 us
    dot_general x20, matrix products, per_device(): lax.dot_general(own_q[:, index * HEAD:(index + 1) * HEAD], key_h, (((1,),...  43.4 us
    select_n x8, other arithmetic, step(): return jax.tree.map(lambda a, b: jnp.where(reached, a, b), new, before)  39.4 us
    mul x24, other arithmetic, expand_part(): wide[:, None, :] * partner * weight[None, :, None]  26.6 us
    unnamed x1, blocking collectives  23.4 us
  transfers between devices with their start and end apart: 4, of which 2 were waited for; matrix products, arithmetic and copies ran while one was open for 24% of the time, Pallas kernels for 0%

commit v1 on v0

v1 whole, which is shorter than its diff:
```python
import jax
import jax.numpy as jnp
from jax import lax
from jax.sharding import PartitionSpec as P

HEAD = 128
GROUP = 5


def per_device(queries, keys, values, log_gate, cand_q, cand_kv, token_ids, fork_pos, slot_map):
    n = lax.axis_size("ctx")
    feats = lax.axis_size("feat")
    me = lax.axis_index("ctx")
    feat = lax.axis_index("feat")
    length = queries.shape[0]
    kv = keys.shape[1] // HEAD
    tri = jnp.tril(jnp.ones((length, length), jnp.float32))
    cumul = jnp.dot(tri, log_gate, precision=lax.Precision.HIGHEST)
    finals = cumul[-1]
    carry = jnp.exp(finals[None, :] - cumul)
    scaled = (
        (carry[:, :, None] * values.reshape(length, kv, HEAD).astype(jnp.float32))
        .astype(jnp.bfloat16)
        .reshape(length, kv * HEAD)
    )
    both = lax.all_gather(jnp.concatenate([keys, scaled], axis=1), "ctx")
    gates = lax.all_gather(cumul, "ctx")
    ends = gates[:, -1, :]
    carries = jnp.exp(ends[:, None, :] - gates)
    rows = length // feats
    start = feat * rows
    q = lax.dynamic_slice_in_dim(queries, start, rows, 0)
    own_cum = lax.dynamic_slice_in_dim(cumul, start, rows, 0)
    causal = (
        lax.broadcasted_iota(jnp.int32, (rows, length), 1)
        <= start + lax.broadcasted_iota(jnp.int32, (rows, length), 0)
    )
    branches = token_ids.shape[0]
    per = branches // (n * feats)
    first = (me * feats + feat) * per
    mine = (first + jnp.arange(per))[:, None] == slot_map[None, :]
    ids = jnp.sum(jnp.where(mine, token_ids[None, :], 0), axis=1)
    forks = jnp.sum(jnp.where(mine, fork_pos[None, :], 0), axis=1)
    pick = (ids[:, None] == jnp.arange(cand_q.shape[0])[None, :]).astype(jnp.bfloat16)
    new_q = jnp.dot(pick, cand_q, preferred_element_type=jnp.float32).astype(jnp.bfloat16)
    new_kv = jnp.einsum("rc,cpd->rpd", pick, cand_kv, preferred_element_type=jnp.float32)
    blocks = jnp.arange(n)

    def between(stop):
        inside = (blocks[None, :] > blocks[:, None]) & (blocks[None, :] < stop)
        total = jnp.sum(jnp.where(inside[:, :, None], ends[None], 0.0), axis=1)
        return jnp.where((blocks < stop)[:, None], jnp.exp(total), 0.0)

    fade_q = between(me)
    fade_b = jnp.stack([between(forks[i]) for i in range(per)])
    outs, bouts = [], []
    for h in range(kv):
        k_own = keys[:, h * HEAD : (h + 1) * HEAD]
        v_own = values[:, h * HEAD : (h + 1) * HEAD]
        k_all = both[:, :, h * HEAD : (h + 1) * HEAD]
        v_all = both[:, :, (kv + h) * HEAD : (kv + h + 1) * HEAD]
        qs = q[:, h * GROUP * HEAD : (h + 1) * GROUP * HEAD].reshape(rows, GROUP, HEAD)
        nq = new_q[:, h * GROUP * HEAD : (h + 1) * GROUP * HEAD].reshape(per, GROUP, HEAD)
        raw = jnp.einsum("tmd,bsd->btms", qs, k_all, preferred_element_type=jnp.float32)
        w = raw * raw
        num = jnp.einsum(
            "btms,bsd->btmd", w.astype(jnp.bfloat16), v_all, preferred_element_type=jnp.float32
        )
        den = jnp.sum(w * carries[:, None, None, :, h], axis=-1)
        growth = jnp.exp(own_cum[:, h])
        a = jnp.sum(num * fade_q[:, None, None, None, h], axis=0) * growth[:, None, None]
        b = jnp.sum(den * fade_q[:, None, None, h], axis=0) * growth[:, None]
        spread = own_cum[:, h][:, None] - cumul[:, h][None, :]
        fading = jnp.where(causal, jnp.exp(jnp.where(causal, spread, 0.0)), 0.0)
        raw = jnp.einsum("tmd,sd->tms", qs, k_own, preferred_element_type=jnp.float32)
        w = raw * raw * fading[:, None, :]
        a = a + jnp.einsum(
            "tms,sd->tmd", w.astype(jnp.bfloat16), v_own, preferred_element_type=jnp.float32
        )
        b = b + jnp.sum(w, axis=-1)
        outs.append(
            (a / HEAD / jnp.maximum(b / HEAD, 1.0)[:, :, None])
            .astype(jnp.bfloat16)
            .reshape(rows, GROUP * HEAD)
        )
        raw = jnp.einsum("rmd,bsd->brms", nq, k_all, preferred_element_type=jnp.float32)
        w = raw * raw
        num = jnp.einsum(
            "brms,bsd->brmd", w.astype(jnp.bfloat16), v_all, preferred_element_type=jnp.float32
        )
        den = jnp.sum(w * carries[:, None, None, :, h], axis=-1)
        fb = fade_b[:, :, h].T
        nk = new_kv[:, 0, h * HEAD : (h + 1) * HEAD].astype(jnp.float32)
        nv = new_kv[:, 1, h * HEAD : (h + 1) * HEAD].astype(jnp.float32)
        inner = jnp.sum(nq.astype(jnp.float32) * nk[:, None, :], axis=-1)
        u = inner * inner
        num = jnp.sum(num * fb[:, :, None, None], axis=0) + u[:, :, None] * nv[:, None, :]
        den = jnp.sum(den * fb[:, :, None], axis=0) + u
        bouts.append(
            (num / HEAD / jnp.maximum(den / HEAD, 1.0)[:, :, None])
            .astype(jnp.bfloat16)
            .reshape(per, GROUP * HEAD)
        )
    return jnp.concatenate(outs, axis=1), jnp.concatenate(bouts, axis=1)


def solution(mesh):
    return jax.shard_map(
        per_device,
        mesh=mesh,
        in_specs=(
            P(("groups", "ctx"), "head"),
            P(("groups", "ctx"), "head"),
            P(("groups", "ctx"), "head"),
            P(("groups", "ctx"), "head"),
            P("groups", "head"),
            P("groups", None, "head"),
            P("groups"),
            P("groups"),
            P("groups"),
        ),
        out_specs=(P(("groups", "ctx", "feat"), "head"), P(("groups", "ctx", "feat"), "head")),
        check_vma=False,
    )
```

time: 862 us -> 58.2 us (0.07); the launches traced: 847 us -> 57.3 us
  waiting for transfers between devices: 367 us -> 13.7 us
  other arithmetic: 171 us -> 5.41 us
  local copies, waits for them, and re-layouts: 105 us -> 4.05 us
  matrix products: 102 us -> 9.1 us
  blocking collectives: 76.8 us -> 10.5 us
  between operations: 25 us -> 14.5 us
    all_gather x1, waiting for transfers between devices: 357 us -> 13.7 us  [per_device(): both = lax.all_gather(jnp.concatenate([keys, scaled], axis=1), 'ctx')]
    dot_general x129 -> x26, matrix products: 102 us -> 8.89 us  [the longest x4 3.54 us: per_device(): jnp.einsum('tmd,bsd->btms', qs, k_all, preferred_element_type=jnp.float32)]
    unnamed x1993 -> x24, local copies, waits for them, and re-layouts: 93.3 us -> 1.79 us
    another operation x30 -> x0, other arithmetic: 59.4 us -> none
    all_gather x2 -> x1, blocking collectives: 53.3 us -> 10.5 us  [per_device(): gates = lax.all_gather(cumul, 'ctx')]
    select_n x9 -> x3, other arithmetic: 39.4 us -> 0.27 us  [the longest x2 0.14 us: between(): return jnp.where((blocks < stop)[:, None], jnp.exp(total), 0.0)]
    mul x24 -> x0, other arithmetic: 26.6 us -> none  [expand_part(): wide[:, None, :] * partner * weight[None, :, None]]
    unnamed x1 -> x0, blocking collectives: 23.4 us -> none
  transfers between devices with their start and end apart: 4 -> 1, of which waited for: 2 -> 1; matrix products, arithmetic and copies ran while one was open for 24% -> 10% of each run, Pallas kernels for 0% -> 0%
where the time goes in v1:
time: 58.2 us; the launch traced here: 57.3 us
  between operations  14.5 us (25%)
  waiting for transfers between devices  13.7 us (24%)
  blocking collectives  10.5 us (18%)
  matrix products  9.1 us (16%)
  other arithmetic  5.41 us (9%)
  local copies, waits for them, and re-layouts  4.05 us (7%)
    all_gather x1, waiting for transfers between devices, per_device(): both = lax.all_gather(jnp.concatenate([keys, scaled], axis=1), 'ctx')  13.7 us
    all_gather x1, blocking collectives, per_device(): gates = lax.all_gather(cumul, 'ctx')  10.5 us
    dot_general x4, matrix products, per_device(): jnp.einsum('tmd,bsd->btms', qs, k_all, preferred_element_type=jnp.float32)  3.54 us
    unnamed x24, local copies, waits for them, and re-layouts  1.79 us
    concatenate x2, other arithmetic, per_device(): return (jnp.concatenate(outs, axis=1), jnp.concatenate(bouts, axis=1))  1.36 us
    lt x3, other arithmetic, between(): return jnp.where((blocks < stop)[:, None], jnp.exp(total), 0.0)  1.35 us
  transfers between devices with their start and end apart: 1, of which 1 were waited for; matrix products, arithmetic and copies ran while one was open for 10% of the time, Pallas kernels for 0%

profile of v1, /device:TPU:1, one launch (start us, length us, event | category | flops | bytes accessed | tf_op | source)
XLA Modules:
  0.0 57.3 jit_solution(13872078565781281476)
XLA Ops:
  7.2 0.9 %fusion.55 = f32[128,4]{0,1:T(4,128)S(1)} fusion(f32[128,4]{0,1:T(4,128)} %param.12), kind=kOutput, calls=%fused_computation.107 | convolution fusion | flops 819200 | bytes 4096 | tf_op jit(solution)/shard_map/dot_general | solution.py:18
  8.1 0.2 slice_reduce_fusion.4
  8.4 0.1 copy.111
  8.6 0.2 mul.540
  8.8 0.7 %copy-done.4 = bf16[128,512]{1,0:T(8,128)(2,1)S(1)} copy-done((bf16[128,512]{1,0:T(8,128)(2,1)S(1)}, bf16[128,512]{1,0:T(8,128)(2,1)}, u32[]{:S(2)}) %copy-start.4) | copy-done | bytes 131096
  9.5 0.9 %copy-done.3 = bf16[128,512]{1,0:T(8,128)(2,1)S(1)} copy-done((bf16[128,512]{1,0:T(8,128)(2,1)S(1)}, bf16[128,512]{1,0:T(8,128)(2,1)}, u32[]{:S(2)}) %copy-start.3) | copy-done | bytes 131096
  10.4 0.7 %pad_maximum_fusion.1 = bf16[128,1024]{1,0:T(8,128)(2,1)} fusion(bf16[128,512]{1,0:T(8,128)(2,1)S(1)} %fusion.36, bf16[128,512]{1,0:T(8,128)(2,1)S(1)} %copy-done.3), kind=kLoop, calls=%fused_computation.68 | loop fusion | flops 524288 | bytes 524288 | tf_op jit(solution)/shard_map/concatenate | solution.py:26
  11.1 10.5 %all-gather.1 = f32[512,4]{0,1:T(4,128)S(1)} all-gather(f32[128,4]{0,1:T(4,128)S(1)} %fusion.55), channel_id=3, replica_groups=mesh['groups'=2,'ctx'=4,'head'=2,'feat'=2] {'ctx'}, dimensions={0}, use_global_device_ids=true | all-gather | bytes 10240 | tf_op jit(solution)/shard_map/all_gather | solution.py:27
  21.7 0.1 copy.151
  21.8 0.1 copy.152
  22.0 0.2 fusion.99
  22.2 0.2 convolution_convert_fusion
  22.5 0.6 %fusion.109 = (s32[1]{0:T(128)}, s32[1]{0:T(128)}) fusion(s32[2]{0:T(128)S(1)} %get-tuple-element.13), kind=kLoop, calls=%fused_computation.254 | loop fusion | bytes 16 | tf_op jit(solution)/shard_map/slice | solution.py:55
  23.1 0.7 %iota_compare_fusion.8 = pred[4]{0:T(512)(128)(4,1)S(1)} fusion(s32[]{:T(128)} %bitcast.53), kind=kLoop, calls=%fused_computation.228 | loop fusion | flops 4 | bytes 8 | tf_op jit(solution)/shard_map/lt | solution.py:52
  23.8 0.7 %iota_compare_fusion.7 = pred[4]{0:T(512)(128)(4,1)S(1)} fusion(s32[]{:T(128)} %bitcast.55), kind=kLoop, calls=%fused_computation.227 | loop fusion | flops 4 | bytes 8 | tf_op jit(solution)/shard_map/lt | solution.py:52
  24.5 0.1 select_reduce_fusion.1
  24.7 0.2 slice_reduce_fusion.3
  25.2 0.1 fusion.86
  25.3 0.1 copy.136
  25.4 0.2 fusion.37
  26.2 0.1 exponential_select_fusion.3
  26.3 0.3 fusion.110
  26.6 0.3 fusion.111
  26.9 0.3 fusion.112
  27.1 0.3 fusion.113
  27.4 13.7 %all-gather.4.cloned.1.call-done = bf16[512,1024]{1,0:T(8,128)(2,1)} async-done(((bf16[128,1024]{1,0:T(8,128)(2,1)}), bf16[512,1024]{1,0:T(8,128)(2,1)}) %all-gather.4.cloned.1.call-update) | async-done | bytes 1048592 | tf_op jit(solution)/shard_map/all_gather | solution.py:26
  41.2 1.4 %multiply_reduce_fusion = (f32[4,64,5]{1,2,0:T(8,128)S(1)}, bf16[4,128,64,5]{1,2,3,0:T(8,128)(2,1)S(1)}) fusion(f32[4,128]{1,0:T(4,128)S(1)} %get-tuple-element.32, bf16[8,5,8,128]{3,2,1,0:T(8,128)(2,1)S(1)} %get-tuple-element.18, bf16[4,128,1024]{2,1,0:T(8,128)(2,1)} %bitcast.318), kind=kOutput, calls=%fused_computation.53 | convolution fusion | flops 42597120 | bytes 547840 | tf_op jit(solution)/shard_map/tmd,bsd->btms/dot_general | solution.py:64
  42.6 1.3 %multiply_reduce_fusion.1 = (f32[4,64,5]{1,2,0:T(8,128)S(1)}, bf16[4,128,64,5]{1,2,3,0:T(8,128)(2,1)S(1)}) fusion(f32[4,128]{1,0:T(4,128)S(1)} %get-tuple-element.33, bf16[8,5,8,128]{3,2,1,0:T(8,128)(2,1)S(1)} %get-tuple-element.16, bf16[4,128,1024]{2,1,0:T(8,128)(2,1)} %bitcast.319), kind=kOutput, calls=%fused_computation.54 | convolution fusion | flops 42597120 | bytes 547840 | tf_op jit(solution)/shard_map/tmd,bsd->btms/dot_general | solution.py:64
  43.9 0.2 fusion.3
  44.2 0.2 fusion.20
  44.4 0.2 fusion.2
  44.7 0.2 fusion.21
  44.9 0.4 multiply_reduce_fusion.2
  45.3 0.4 multiply_reduce_fusion.3
  45.7 0.2 fusion.1
  46.0 0.2 fusion.22
  46.2 0.2 fusion
  46.5 0.2 fusion.23
  46.7 0.2 multiply_reduce_fusion.4
  47.0 0.1 fusion.27
  47.3 0.2 multiply_reduce_fusion.5
  47.6 0.1 fusion.26
  47.9 0.2 multiply_reduce_fusion.6
  48.2 0.1 fusion.25
  48.5 0.2 multiply_reduce_fusion.7
  48.8 0.1 fusion.24
  49.1 0.8 %pad_maximum_fusion = bf16[64,2560]{1,0:T(8,128)(2,1)} fusion(bf16[64,640]{1,0:T(8,128)(2,1)S(1)} %bitcast.314, bf16[64,640]{1,0:T(8,128)(2,1)S(1)} %bitcast.315, bf16[64,640]{1,0:T(8,128)(2,1)S(1)} %bitcast.316, bf16[64,640]{1,0:T(8,128)(2,1)S(1)} %bitcast.317), kind=kLoop, calls=%fused_computation.57 | loop fusion | flops 1310720 | bytes 655360 | tf_op jit(solution)/shard_map/concatenate | solution.py:104
  49.8 0.6 %pad_maximum_fusion.2 = bf16[2,2560]{1,0:T(2,128)(2,1)} fusion(bf16[2,640]{1,0:T(2,128)(2,1)S(1)} %bitcast.334, bf16[2,640]{1,0:T(2,128)(2,1)S(1)} %bitcast.335, bf16[2,640]{1,0:T(2,128)(2,1)S(1)} %bitcast.336, bf16[2,640]{1,0:T(2,128)(2,1)S(1)} %bitcast.337), kind=kLoop, calls=%fused_computation.149 | loop fusion | flops 40960 | bytes 20480 | tf_op jit(solution)/shard_map/concatenate | solution.py:104
  (78 shorter events, 2.3 us)
Async XLA Ops:
  7.2 15.0 %copy-start = (bf16[64,2560]{1,0:T(8,128)(2,1)S(1)}, bf16[64,2560]{1,0:T(8,128)(2,1)}, u32[]{:S(2)}) copy-start(bf16[64,2560]{1,0:T(8,128)(2,1)} %param.13) | copy-start | bytes 983044
  7.2 34.0 %all-gather.4.cloned.1.call-start = ((), (), s32[]{:S(2)}) async-start(), calls=%async_computation | async-start | bytes 1310720 | tf_op jit(solution)/shard_map/all_gather | solution.py:26
  8.5 0.9 %copy-start.4 = (bf16[128,512]{1,0:T(8,128)(2,1)S(1)}, bf16[128,512]{1,0:T(8,128)(2,1)}, u32[]{:S(2)}) copy-start(bf16[128,512]{1,0:T(8,128)(2,1)} %param.11) | copy-start | bytes 393220
  9.5 0.9 %copy-start.3 = (bf16[128,512]{1,0:T(8,128)(2,1)S(1)}, bf16[128,512]{1,0:T(8,128)(2,1)}, u32[]{:S(2)}) copy-start(bf16[128,512]{1,0:T(8,128)(2,1)} %param.10) | copy-start | bytes 393220
  10.4 11.6 %copy-start.5 = (s32[16]{0:T(128)S(1)}, s32[16]{0:T(128)}, u32[]{:S(2)}) copy-start(s32[16]{0:T(128)} %param.16) | copy-start | bytes 196
  10.4 11.6 %copy-start.6 = (s32[16]{0:T(128)S(1)}, s32[16]{0:T(128)}, u32[]{:S(2)}) copy-start(s32[16]{0:T(128)} %param.17) | copy-start | bytes 196
  10.4 11.6 %copy-start.7 = (s32[16]{0:T(128)S(1)}, s32[16]{0:T(128)}, u32[]{:S(2)}) copy-start(s32[16]{0:T(128)} %param.15) | copy-start | bytes 196
  11.1 14.8 %copy-start.2 = (bf16[128,2560]{1,0:T(8,128)(2,1)S(1)}, bf16[128,2560]{1,0:T(8,128)(2,1)}, u32[]{:S(2)}) copy-start(bf16[128,2560]{1,0:T(8,128)(2,1)} %param.9) | copy-start | bytes 1966084
  22.4 3.1 %copy-start.8 = (bf16[64,2,512]{2,1,0:T(2,128)(2,1)S(1)}, bf16[64,2,512]{2,1,0:T(2,128)(2,1)}, u32[]{:S(2)}) copy-start(bf16[64,2,512]{2,1,0:T(2,128)(2,1)} %param.14) | copy-start | bytes 393220
  41.2 2.7 %copy-start.1 = (bf16[512,1024]{1,0:T(8,128)(2,1)S(1)}, bf16[512,1024]{1,0:T(8,128)(2,1)}, u32[]{:S(2)}) copy-start(bf16[512,1024]{1,0:T(8,128)(2,1)} %all-gather.4.cloned.1.call-done) | copy-start | bytes 3145732
Sparse Core Ops, SparseCore 0:
  11.2 29.8 all-gather.3

commit v2 on v1

v2 whole, which is shorter than its diff:
```python
import functools

import jax
import jax.numpy as jnp
from jax import lax
from jax.experimental import pallas as pl
from jax.experimental.pallas import tpu as pltpu
from jax.sharding import PartitionSpec as P

HEAD = 128
GROUP = 5
F32, BF16 = jnp.float32, jnp.bfloat16
MESH = pl.DeviceIdType.MESH


def dot_t(a, b, **kw):
    return lax.dot_general(a, b, (((1,), (1,)), ((), ())), preferred_element_type=F32, **kw)


def kernel(
    n, feats, q_ref, k_ref, v_ref, g_ref, cq_ref, ckv_ref, ids_ref, fork_ref, slot_ref,
    out_ref, bout_ref, buf, gbuf, gcol, num, den, bscr,
    g_send, g_recv, z_send, z_recv, s_send, s_recv,
):
    me, feat = lax.axis_index("ctx"), lax.axis_index("feat")
    length = q_ref.shape[0]
    rows = length // feats
    kv = k_ref.shape[1] // HEAD
    start = pl.multiple_of(feat * rows, rows)
    count = ids_ref.shape[0]
    per = count // (n * feats)
    tall, wide = GROUP * rows, 8 * per

    barrier = pltpu.get_barrier_semaphore()
    for d in range(1, n):
        pl.semaphore_signal(
            barrier, inc=1, device_id={"ctx": lax.rem(me + d, n)}, device_id_type=MESH
        )
    for o in range(1, feats):
        pl.semaphore_signal(
            barrier, inc=1, device_id={"feat": lax.rem(feat + o, feats)}, device_id_type=MESH
        )

    r = lax.broadcasted_iota(jnp.int32, (length, length), 0)
    c = lax.broadcasted_iota(jnp.int32, (length, length), 1)
    tri = (c <= r).astype(F32)
    gates = g_ref[...]
    g_lane = dot_t(gates, tri, precision=lax.Precision.HIGHEST)
    g_row = dot_t(tri, gates, precision=lax.Precision.HIGHEST)
    gcol[...] = g_row
    gbuf[me] = jnp.zeros(gbuf.shape[1:], F32)
    gbuf[me, 0:kv, :] = g_lane
    carry = jnp.exp(g_row[length - 1 : length, :] - g_row)
    buf[me, 0] = k_ref[...]
    for h in range(kv):
        cols = slice(h * HEAD, (h + 1) * HEAD)
        buf[me, 1, :, cols] = (carry[:, h : h + 1] * v_ref[:, cols].astype(F32)).astype(BF16)

    pl.semaphore_wait(barrier, n - 1 + feats - 1)
    sends, gsends = [], []
    for d in range(1, n):
        there = {"ctx": lax.rem(me + d, n)}
        gsends.append(
            pltpu.make_async_remote_copy(
                src_ref=gbuf.at[me], dst_ref=gbuf.at[me], send_sem=g_send.at[d - 1],
                recv_sem=g_recv.at[d - 1], device_id=there, device_id_type=MESH,
            )
        )
        gsends[-1].start()
    for d in range(1, n):
        there = {"ctx": lax.rem(me + d, n)}
        part = buf.at[me, :, pl.ds(start, rows), :]
        sends.append(
            pltpu.make_async_remote_copy(
                src_ref=part, dst_ref=part, send_sem=z_send.at[d - 1],
                recv_sem=z_recv.at[d - 1], device_id=there, device_id_type=MESH,
            )
        )
        sends[-1].start()

    first = (me * feats + feat) * per
    ids, forks = [], []
    for i in range(per):
        a = b = jnp.int32(0)
        for s in range(count):
            hit = slot_ref[s] == first + i
            a = a + jnp.where(hit, ids_ref[s], 0)
            b = b + jnp.where(hit, fork_ref[s], 0)
        ids.append(a)
        forks.append(b)
    cands = cq_ref.shape[0]
    line = lax.broadcasted_iota(jnp.int32, (wide, cands), 0)
    place = lax.broadcasted_iota(jnp.int32, (wide, cands), 1)
    wanted = jnp.zeros((wide, cands), jnp.int32)
    brow = lax.broadcasted_iota(jnp.int32, (wide, 1), 0)
    stop = jnp.zeros((wide, 1), jnp.int32)
    for i in range(per):
        wanted = jnp.where(line >= 8 * i, ids[i], wanted)
        stop = jnp.where(brow >= 8 * i, forks[i], stop)
    pick = jnp.where(place == wanted, 1.0, 0.0).astype(BF16)
    new_kv = [ckv_ref[ids[i]].astype(F32) for i in range(per)]
    member = lax.broadcasted_iota(jnp.int32, (wide, HEAD), 0) % 8

    own_g = gcol[pl.ds(start, rows), :]
    t_at = start + lax.broadcasted_iota(jnp.int32, (rows, length), 0)
    causal = lax.broadcasted_iota(jnp.int32, (rows, length), 1) <= t_at
    stacked, new_q = [], []
    for h in range(kv):
        cols = slice(h * HEAD, (h + 1) * HEAD)
        base = h * GROUP * HEAD
        qs = jnp.concatenate(
            [q_ref[pl.ds(start, rows), base + m * HEAD : base + (m + 1) * HEAD] for m in range(GROUP)],
            axis=0,
        )
        nq = jnp.zeros((wide, HEAD), F32)
        for m in range(GROUP):
            got = jnp.dot(
                pick, cq_ref[:, base + m * HEAD : base + (m + 1) * HEAD], preferred_element_type=F32
            )
            nq = jnp.where(member == m, got, nq)
        new_q.append(nq)
        stacked.append(jnp.concatenate([qs, nq.astype(BF16)], axis=0))
        fading = jnp.where(
            causal,
            jnp.exp(jnp.where(causal, own_g[:, h : h + 1] - g_lane[h : h + 1, :], 0.0)),
            0.0,
        )
        raw = dot_t(qs, k_ref[:, cols])
        w = raw * raw * jnp.concatenate([fading] * GROUP, axis=0)
        num[h, 0:tall, :] = jnp.dot(w.astype(BF16), v_ref[:, cols], preferred_element_type=F32)
        den[h, 0:tall, :] = w
        nk = jnp.concatenate(
            [jnp.broadcast_to(x[0:1, cols], (8, HEAD)) for x in new_kv], axis=0
        )
        nv = jnp.concatenate(
            [jnp.broadcast_to(x[1:2, cols], (8, HEAD)) for x in new_kv], axis=0
        )
        inner = jnp.sum(nq * nk, axis=1, keepdims=True)
        u = inner * inner
        num[h, tall : tall + wide, :] = u * nv
        den[h, tall : tall + wide, :] = jnp.broadcast_to(u * (1.0 / HEAD), (wide, HEAD))

    for copy in gsends:
        copy.wait_recv()

    def decays(src, h):
        total_q = jnp.zeros((1, 1), F32)
        total_b = jnp.zeros((wide, 1), F32)
        for j in range(1, n):
            end = gbuf[j, h : h + 1, length - 1 : length]
            after = jnp.where(j > src, end, jnp.zeros_like(end))
            total_q = total_q + jnp.where(j < me, after, jnp.zeros_like(after))
            total_b = total_b + jnp.where(stop > j, after, 0.0)
        fade_q = jnp.exp(total_q) * jnp.where(src < me, 1.0, 0.0)
        fade_b = jnp.where(stop > src, jnp.exp(total_b), 0.0)
        return fade_q, fade_b

    def add(src, h, own):
        cols = slice(h * HEAD, (h + 1) * HEAD)
        fade_q, fade_b = decays(src, h)
        lanes = gbuf[src, h : h + 1, :]
        keep = jnp.exp(lanes[:, length - 1 : length] - lanes)
        lhs = new_q[h].astype(BF16) if own else stacked[h]
        raw = dot_t(lhs, buf[src, 0, :, cols])
        w = raw * raw
        got = jnp.dot(w.astype(BF16), buf[src, 1, :, cols], preferred_element_type=F32)
        w = w * keep
        if own:
            num[h, tall : tall + wide, :] += fade_b * got
            den[h, tall : tall + wide, :] += fade_b * w
            return
        grow = jnp.exp(own_g[:, h : h + 1]) * fade_q
        weight = jnp.concatenate([grow] * GROUP + [fade_b], axis=0)
        num[h] += weight * got
        den[h] += weight * w

    for h in range(kv):
        add(me, h, True)

    passed = []
    for d in range(1, n):
        src = lax.rem(me - d + n, n)
        sends[d - 1].wait_recv()
        part = buf.at[src, :, pl.ds(start, rows), :]
        hops = []
        for o in range(1, feats):
            copy = pltpu.make_async_remote_copy(
                src_ref=part, dst_ref=part, send_sem=s_send.at[d - 1, o - 1],
                recv_sem=s_recv.at[d - 1, o - 1],
                device_id={"feat": lax.rem(feat + o, feats)}, device_id_type=MESH,
            )
            copy.start()
            hops.append(copy)
        passed += hops
        for copy in hops:
            copy.wait_recv()
        for h in range(kv):
            add(src, h, False)

    for h in range(kv):
        total = jnp.sum(den[h], axis=1, keepdims=True) * (1.0 / HEAD)
        res = num[h] * (1.0 / HEAD) / jnp.maximum(total, 1.0)
        base = h * GROUP * HEAD
        for m in range(GROUP):
            cols = slice(base + m * HEAD, base + (m + 1) * HEAD)
            out_ref[:, cols] = res[m * rows : (m + 1) * rows].astype(BF16)
            for i in range(per):
                at = tall + 8 * i + m
                bscr[i : i + 1, cols] = res[at : at + 1]
    bout_ref[...] = bscr[...].astype(BF16)
    for copy in gsends + sends + passed:
        copy.wait_send()


def per_device(queries, keys, values, log_gate, cand_q, cand_kv, token_ids, fork_pos, slot_map):
    n, feats = lax.axis_size("ctx"), lax.axis_size("feat")
    length, width = queries.shape
    kv = keys.shape[1] // HEAD
    rows = length // feats
    per = token_ids.shape[0] // (n * feats)
    tall = GROUP * rows + 8 * per
    vmem, smem = pl.BlockSpec(memory_space=pltpu.VMEM), pl.BlockSpec(memory_space=pltpu.SMEM)
    dma = pltpu.SemaphoreType.DMA
    return pl.pallas_call(
        functools.partial(kernel, n, feats),
        out_shape=(
            jax.ShapeDtypeStruct((rows, width), BF16),
            jax.ShapeDtypeStruct((per, width), BF16),
        ),
        in_specs=[vmem] * 6 + [smem] * 3,
        out_specs=(vmem, vmem),
        scratch_shapes=[
            pltpu.VMEM((n, 2, length, kv * HEAD), BF16),
            pltpu.VMEM((n, -(-kv // 8) * 8, length), F32),
            pltpu.VMEM((length, kv), F32),
            pltpu.VMEM((kv, tall, HEAD), F32),
            pltpu.VMEM((kv, tall, HEAD), F32),
            pltpu.VMEM((per, width), F32),
            dma((n - 1,)), dma((n - 1,)), dma((n - 1,)), dma((n - 1,)),
            dma((n - 1, feats - 1)), dma((n - 1, feats - 1)),
        ],
        compiler_params=pltpu.CompilerParams(
            collective_id=0, has_side_effects=True, vmem_limit_bytes=40 * 2**20
        ),
    )(queries, keys, values, log_gate.T, cand_q, cand_kv, token_ids, fork_pos, slot_map)


def solution(mesh):
    return jax.shard_map(
        per_device,
        mesh=mesh,
        in_specs=(
            P(("groups", "ctx"), "head"),
            P(("groups", "ctx"), "head"),
            P(("groups", "ctx"), "head"),
            P(("groups", "ctx"), "head"),
            P("groups", "head"),
            P("groups", None, "head"),
            P("groups"),
            P("groups"),
            P("groups"),
        ),
        out_specs=(P(("groups", "ctx", "feat"), "head"), P(("groups", "ctx", "feat"), "head")),
        check_vma=False,
    )
```

time: 58.2 us -> 28.2 us (0.48)
  the two profiles are of different devices: /device:TPU:1 before, /device:TPU:19 now
where the time goes in v2:
time: 28.2 us; the launch traced here: 27.9 us
  Pallas kernels  19.8 us (70%)
  local copies, waits for them, and re-layouts  7.44 us (26%)
  between operations  0.67 us (2%)
    pallas_call x1, Pallas kernels, per_device(): pl.pallas_call(functools.partial(kernel, n, feats), out_shape=(jax.ShapeD...  19.8 us
    unnamed x20, local copies, waits for them, and re-layouts  7.44 us

profile of v2, /device:TPU:19, one launch (start us, length us, event | category | flops | bytes accessed | tf_op | source)
XLA Modules:
  0.0 27.9 jit_solution(14764297716325587081)
XLA Ops:
  0.6 0.0 copy-start.8
  0.6 0.0 copy-start.7
  0.7 0.0 copy-start.6
  0.7 0.6 %copy-done.8 = s32[16]{0:T(128)S(1)} copy-done((s32[16]{0:T(128)S(1)}, s32[16]{0:T(128)}, u32[]{:S(2)}) %copy-start.8) | copy-done | bytes 88
  1.3 0.0 copy-done.7
  1.3 0.0 copy-done.6
  1.3 0.0 copy-start
  1.3 1.1 %copy-done = bf16[128,2560]{1,0:T(8,128)(2,1)S(1)} copy-done((bf16[128,2560]{1,0:T(8,128)(2,1)S(1)}, bf16[128,2560]{1,0:T(8,128)(2,1)}, u32[]{:S(2)}) %copy-start) | copy-done | bytes 655384
  2.4 0.0 copy-start.1
  2.4 1.0 %copy-done.1 = bf16[64,2560]{1,0:T(8,128)(2,1)S(1)} copy-done((bf16[64,2560]{1,0:T(8,128)(2,1)S(1)}, bf16[64,2560]{1,0:T(8,128)(2,1)}, u32[]{:S(2)}) %copy-start.1) | copy-done | bytes 327704
  3.4 0.0 copy-start.2
  3.4 0.9 %copy-done.2 = bf16[128,512]{1,0:T(8,128)(2,1)S(1)} copy-done((bf16[128,512]{1,0:T(8,128)(2,1)S(1)}, bf16[128,512]{1,0:T(8,128)(2,1)}, u32[]{:S(2)}) %copy-start.2) | copy-done | bytes 131096
  4.3 0.0 copy-start.3
  4.3 0.9 %copy-done.3 = bf16[128,512]{1,0:T(8,128)(2,1)S(1)} copy-done((bf16[128,512]{1,0:T(8,128)(2,1)S(1)}, bf16[128,512]{1,0:T(8,128)(2,1)}, u32[]{:S(2)}) %copy-start.3) | copy-done | bytes 131096
  5.2 0.0 copy-start.4
  5.2 0.9 %copy-done.4 = bf16[64,2,512]{2,1,0:T(2,128)(2,1)S(1)} copy-done((bf16[64,2,512]{2,1,0:T(2,128)(2,1)S(1)}, bf16[64,2,512]{2,1,0:T(2,128)(2,1)}, u32[]{:S(2)}) %copy-start.4) | copy-done | bytes 131096
  6.1 0.0 copy-start.5
  6.1 0.7 %copy-done.5 = f32[128,4]{0,1:T(4,128)S(1)} copy-done((f32[128,4]{0,1:T(4,128)S(1)}, f32[128,4]{0,1:T(4,128)}, u32[]{:S(2)}) %copy-start.5) | copy-done | bytes 2072
  6.8 19.8 %shard_map.104 = (bf16[64,2560]{1,0:T(8,128)(2,1)S(1)}, bf16[2,2560]{1,0:T(2,128)(2,1)S(1)}) custom-call(bf16[128,2560]{1,0:T(8,128)(2,1)S(1)} %copy-done, bf16[128,512]{1,0:T(8,128)(2,1)S(1)} %copy-done.2, bf16[128,512]{1,0:T(8,128)(2,1)S(1)} %copy-done.3, f32[4,128]{1,0:T(4,128)S(1)} %bitcast.1, bf16[64,2560]{1,0:T(8,128)(2,1)S(1)} %copy-done.1, ...), custom_call_target="tpu_custom_call" | custom-call | tf_op jit(solution)/shard_map/pallas_call | solution.py:224
  26.5 0.7 %copy.13 = bf16[64,2560]{1,0:T(8,128)(2,1)} copy(bf16[64,2560]{1,0:T(8,128)(2,1)S(1)} %get-tuple-element.4) | data formatting | bytes 655360
  27.3 0.6 %copy.14 = bf16[2,2560]{1,0:T(2,128)(2,1)} copy(bf16[2,2560]{1,0:T(2,128)(2,1)S(1)} %get-tuple-element.5) | data formatting | bytes 20480
Async XLA Ops:
  0.6 0.7 %copy-start.8 = (s32[16]{0:T(128)S(1)}, s32[16]{0:T(128)}, u32[]{:S(2)}) copy-start(s32[16]{0:T(128)} %slot_ref.1) | copy-start | bytes 196
  0.6 0.7 %copy-start.7 = (s32[16]{0:T(128)S(1)}, s32[16]{0:T(128)}, u32[]{:S(2)}) copy-start(s32[16]{0:T(128)} %fork_ref.1) | copy-start | bytes 196
  0.7 0.7 %copy-start.6 = (s32[16]{0:T(128)S(1)}, s32[16]{0:T(128)}, u32[]{:S(2)}) copy-start(s32[16]{0:T(128)} %ids_ref.1) | copy-start | bytes 196
  1.3 1.1 %copy-start = (bf16[128,2560]{1,0:T(8,128)(2,1)S(1)}, bf16[128,2560]{1,0:T(8,128)(2,1)}, u32[]{:S(2)}) copy-start(bf16[128,2560]{1,0:T(8,128)(2,1)} %q_ref.1) | copy-start | bytes 1966084
  2.4 1.0 %copy-start.1 = (bf16[64,2560]{1,0:T(8,128)(2,1)S(1)}, bf16[64,2560]{1,0:T(8,128)(2,1)}, u32[]{:S(2)}) copy-start(bf16[64,2560]{1,0:T(8,128)(2,1)} %cq_ref.1) | copy-start | bytes 983044
  3.4 0.9 %copy-start.2 = (bf16[128,512]{1,0:T(8,128)(2,1)S(1)}, bf16[128,512]{1,0:T(8,128)(2,1)}, u32[]{:S(2)}) copy-start(bf16[128,512]{1,0:T(8,128)(2,1)} %k_ref.1) | copy-start | bytes 393220
  4.3 0.9 %copy-start.3 = (bf16[128,512]{1,0:T(8,128)(2,1)S(1)}, bf16[128,512]{1,0:T(8,128)(2,1)}, u32[]{:S(2)}) copy-start(bf16[128,512]{1,0:T(8,128)(2,1)} %v_ref.1) | copy-start | bytes 393220
  5.2 0.9 %copy-start.4 = (bf16[64,2,512]{2,1,0:T(2,128)(2,1)S(1)}, bf16[64,2,512]{2,1,0:T(2,128)(2,1)}, u32[]{:S(2)}) copy-start(bf16[64,2,512]{2,1,0:T(2,128)(2,1)} %ckv_ref.1) | copy-start | bytes 393220
  6.1 0.7 %copy-start.5 = (f32[128,4]{0,1:T(4,128)S(1)}, f32[128,4]{0,1:T(4,128)}, u32[]{:S(2)}) copy-start(f32[128,4]{0,1:T(4,128)} %param.12) | copy-start | bytes 6148

commit v3 on v2

--- a/solution.py
+++ b/solution.py
@@ -18,14 +18,16 @@
 
 
 def kernel(
-    n, feats, q_ref, k_ref, v_ref, g_ref, cq_ref, ckv_ref, ids_ref, fork_ref, slot_ref,
-    out_ref, bout_ref, buf, gbuf, gcol, num, den, bscr,
-    g_send, g_recv, z_send, z_recv, s_send, s_recv,
+    n, feats, q_hbm, k_hbm, v_hbm, g_hbm, cq_hbm, ckv_hbm, ids_hbm, fork_hbm, slot_hbm,
+    out_ref, bout_ref, q_ref, v_ref, g_ref, cq_ref, ckv_ref, ids_ref, fork_ref, slot_ref,
+    buf, gbuf, gcol, num, den, bscr,
+    l_sem, g_send, g_recv, z_send, z_recv, s_send, s_recv,
 ):
     me, feat = lax.axis_index("ctx"), lax.axis_index("feat")
-    length = q_ref.shape[0]
+    length = q_hbm.shape[0]
     rows = length // feats
-    kv = k_ref.shape[1] // HEAD
+    kv = k_hbm.shape[1] // HEAD
+    up, down = me < n - 1, me > 0
     start = pl.multiple_of(feat * rows, rows)
     count = ids_ref.shape[0]
     per = count // (n * feats)
@@ -41,6 +43,19 @@
             barrier, inc=1, device_id={"feat": lax.rem(feat + o, feats)}, device_id_type=MESH
         )
 
+    loads = [
+        pltpu.make_async_copy(src, dst, l_sem.at[i])
+        for i, (src, dst) in enumerate(
+            [
+                (g_hbm, g_ref), (v_hbm, v_ref), (k_hbm, buf.at[me, 0]),
+                (q_hbm.at[pl.ds(start, rows), :], q_ref), (cq_hbm, cq_ref), (ckv_hbm, ckv_ref),
+                (ids_hbm, ids_ref), (fork_hbm, fork_ref), (slot_hbm, slot_ref),
+            ]
+        )
+    ]
+    for copy in loads:
+        copy.start()
+    loads[0].wait()
     r = lax.broadcasted_iota(jnp.int32, (length, length), 0)
     c = lax.broadcasted_iota(jnp.int32, (length, length), 1)
     tri = (c <= r).astype(F32)
@@ -51,13 +66,46 @@
     gbuf[me] = jnp.zeros(gbuf.shape[1:], F32)
     gbuf[me, 0:kv, :] = g_lane
     carry = jnp.exp(g_row[length - 1 : length, :] - g_row)
-    buf[me, 0] = k_ref[...]
-    for h in range(kv):
-        cols = slice(h * HEAD, (h + 1) * HEAD)
-        buf[me, 1, :, cols] = (carry[:, h : h + 1] * v_ref[:, cols].astype(F32)).astype(BF16)
-
+    def along(side, d, part):
+        block = me - (d - 1) if side == 0 else me + (d - 1)
+        ref = buf.at[block, part, pl.ds(start, rows), :]
+        at = (side * (n - 1) + d - 1) * 2 + part
+        return pltpu.make_async_remote_copy(
+            src_ref=ref, dst_ref=ref, send_sem=z_send.at[at], recv_sem=z_recv.at[at],
+            device_id={"ctx": me + 1 if side == 0 else me - 1}, device_id_type=MESH,
+        )
+
+    def arrival(side, d, part):
+        block = me - d if side == 0 else me + d
+        ref = buf.at[block, part, pl.ds(start, rows), :]
+        at = (side * (n - 1) + d - 1) * 2 + part
+        return pltpu.make_async_remote_copy(
+            src_ref=ref, dst_ref=ref, send_sem=z_send.at[at], recv_sem=z_recv.at[at],
+            device_id={"ctx": me - 1 if side == 0 else me + 1}, device_id_type=MESH,
+        )
+
+    def across(side, d, part):
+        block = me - d if side == 0 else me + d
+        ref = buf.at[block, part, pl.ds(start, rows), :]
+        at = ((side * (n - 1) + d - 1) * 2 + part) * (feats - 1)
+        return [
+            pltpu.make_async_remote_copy(
+                src_ref=ref, dst_ref=ref, send_sem=s_send.at[at + o - 1],
+                recv_sem=s_recv.at[at + o - 1],
+                device_id={"feat": lax.rem(feat + o, feats)}, device_id_type=MESH,
+            )
+            for o in range(1, feats)
+        ]
+
+    def sends(side, d):
+        return (up if side == 0 else down) & arrives(side, d - 1)
+
+    def arrives(side, d):
+        return me >= d if side == 0 else me + d < n
+
+    loads[2].wait()
     pl.semaphore_wait(barrier, n - 1 + feats - 1)
-    sends, gsends = [], []
+    gsends = []
     for d in range(1, n):
         there = {"ctx": lax.rem(me + d, n)}
         gsends.append(
@@ -67,16 +115,20 @@
             )
         )
         gsends[-1].start()
-    for d in range(1, n):
-        there = {"ctx": lax.rem(me + d, n)}
-        part = buf.at[me, :, pl.ds(start, rows), :]
-        sends.append(
-            pltpu.make_async_remote_copy(
-                src_ref=part, dst_ref=part, send_sem=z_send.at[d - 1],
-                recv_sem=z_recv.at[d - 1], device_id=there, device_id_type=MESH,
-            )
-        )
-        sends[-1].start()
+    for side in range(2):
+        @pl.when(sends(side, 1))
+        def _(side=side):
+            along(side, 1, 0).start()
+    loads[1].wait()
+    for h in range(kv):
+        cols = slice(h * HEAD, (h + 1) * HEAD)
+        buf[me, 1, :, cols] = (carry[:, h : h + 1] * v_ref[:, cols].astype(F32)).astype(BF16)
+    for side in range(2):
+        @pl.when(sends(side, 1))
+        def _(side=side):
+            along(side, 1, 1).start()
+    for copy in loads[3:]:
+        copy.wait()
 
     first = (me * feats + feat) * per
     ids, forks = [], []
@@ -109,7 +161,7 @@
         cols = slice(h * HEAD, (h + 1) * HEAD)
         base = h * GROUP * HEAD
         qs = jnp.concatenate(
-            [q_ref[pl.ds(start, rows), base + m * HEAD : base + (m + 1) * HEAD] for m in range(GROUP)],
+            [q_ref[:, base + m * HEAD : base + (m + 1) * HEAD] for m in range(GROUP)],
             axis=0,
         )
         nq = jnp.zeros((wide, HEAD), F32)
@@ -125,7 +177,7 @@
             jnp.exp(jnp.where(causal, own_g[:, h : h + 1] - g_lane[h : h + 1, :], 0.0)),
             0.0,
         )
-        raw = dot_t(qs, k_ref[:, cols])
+        raw = dot_t(qs, buf[me, 0, :, cols])
         w = raw * raw * jnp.concatenate([fading] * GROUP, axis=0)
         num[h, 0:tall, :] = jnp.dot(w.astype(BF16), v_ref[:, cols], preferred_element_type=F32)
         den[h, 0:tall, :] = w
@@ -155,7 +207,7 @@
         fade_b = jnp.where(stop > src, jnp.exp(total_b), 0.0)
         return fade_q, fade_b
 
-    def add(src, h, own):
+    def add(src, h, own=False):
         cols = slice(h * HEAD, (h + 1) * HEAD)
         fade_q, fade_b = decays(src, h)
         lanes = gbuf[src, h : h + 1, :]
@@ -177,25 +229,26 @@
     for h in range(kv):
         add(me, h, True)
 
-    passed = []
     for d in range(1, n):
-        src = lax.rem(me - d + n, n)
-        sends[d - 1].wait_recv()
-        part = buf.at[src, :, pl.ds(start, rows), :]
-        hops = []
-        for o in range(1, feats):
-            copy = pltpu.make_async_remote_copy(
-                src_ref=part, dst_ref=part, send_sem=s_send.at[d - 1, o - 1],
-                recv_sem=s_recv.at[d - 1, o - 1],
-                device_id={"feat": lax.rem(feat + o, feats)}, device_id_type=MESH,
-            )
-            copy.start()
-            hops.append(copy)
-        passed += hops
-        for copy in hops:
-            copy.wait_recv()
-        for h in range(kv):
-            add(src, h, False)
+        for side in range(2):
+            @pl.when(arrives(side, d))
+            def _(side=side, d=d):
+                for part in range(2):
+                    arrival(side, d, part).wait_recv()
+                    if d < n - 1:
+                        @pl.when(sends(side, d + 1))
+                        def _():
+                            along(side, d + 1, part).start()
+                    for copy in across(side, d, part):
+                        copy.start()
+        for side in range(2):
+            @pl.when(arrives(side, d))
+            def _(side=side, d=d):
+                for part in range(2):
+                    for copy in across(side, d, part):
+                        copy.wait_recv()
+                for h in range(kv):
+                    add(me - d if side == 0 else me + d, h, side == 1)
 
     for h in range(kv):
         total = jnp.sum(den[h], axis=1, keepdims=True) * (1.0 / HEAD)
@@ -208,8 +261,20 @@
                 at = tall + 8 * i + m
                 bscr[i : i + 1, cols] = res[at : at + 1]
     bout_ref[...] = bscr[...].astype(BF16)
-    for copy in gsends + sends + passed:
+    for copy in gsends:
         copy.wait_send()
+    for d in range(1, n):
+        for side in range(2):
+            @pl.when(sends(side, d))
+            def _(side=side, d=d):
+                for part in range(2):
+                    along(side, d, part).wait_send()
+
+            @pl.when(arrives(side, d))
+            def _(side=side, d=d):
+                for part in range(2):
+                    for copy in across(side, d, part):
+                        copy.wait_send()
 
 
 def per_device(queries, keys, values, log_gate, cand_q, cand_kv, token_ids, fork_pos, slot_map):
@@ -219,7 +284,8 @@
     rows = length // feats
     per = token_ids.shape[0] // (n * feats)
     tall = GROUP * rows + 8 * per
-    vmem, smem = pl.BlockSpec(memory_space=pltpu.VMEM), pl.BlockSpec(memory_space=pltpu.SMEM)
+    vmem, hbm = pl.BlockSpec(memory_space=pltpu.VMEM), pl.BlockSpec(memory_space=pltpu.HBM)
+    hops = 2 * (n - 1) * 2
     dma = pltpu.SemaphoreType.DMA
     return pl.pallas_call(
         functools.partial(kernel, n, feats),
@@ -227,17 +293,25 @@
             jax.ShapeDtypeStruct((rows, width), BF16),
             jax.ShapeDtypeStruct((per, width), BF16),
         ),
-        in_specs=[vmem] * 6 + [smem] * 3,
+        in_specs=[hbm] * 9,
         out_specs=(vmem, vmem),
         scratch_shapes=[
+            pltpu.VMEM((rows, width), BF16),
+            pltpu.VMEM(values.shape, BF16),
+            pltpu.VMEM((kv, length), F32),
+            pltpu.VMEM(cand_q.shape, BF16),
+            pltpu.VMEM(cand_kv.shape, BF16),
+            pltpu.SMEM(token_ids.shape, jnp.int32),
+            pltpu.SMEM(fork_pos.shape, jnp.int32),
+            pltpu.SMEM(slot_map.shape, jnp.int32),
             pltpu.VMEM((n, 2, length, kv * HEAD), BF16),
             pltpu.VMEM((n, -(-kv // 8) * 8, length), F32),
             pltpu.VMEM((length, kv), F32),
             pltpu.VMEM((kv, tall, HEAD), F32),
             pltpu.VMEM((kv, tall, HEAD), F32),
             pltpu.VMEM((per, width), F32),
-            dma((n - 1,)), dma((n - 1,)), dma((n - 1,)), dma((n - 1,)),
-            dma((n - 1, feats - 1)), dma((n - 1, feats - 1)),
+            dma((9,)), dma((n - 1,)), dma((n - 1,)), dma((hops,)), dma((hops,)),
+            dma((hops * (feats - 1),)), dma((hops * (feats - 1),)),
         ],
         compiler_params=pltpu.CompilerParams(
             collective_id=0, has_side_effects=True, vmem_limit_bytes=40 * 2**20

time: 28.2 us -> 27.7 us (0.982)
  the two profiles are of different devices: /device:TPU:19 before, /device:TPU:1 now
where the time goes in v3:
time: 27.7 us; the launch traced here: 27.4 us
  Pallas kernels  19.3 us (70%)
  local copies, waits for them, and re-layouts  7.44 us (27%)
  between operations  0.67 us (2%)
    pallas_call x1, Pallas kernels, per_device(): pl.pallas_call(functools.partial(kernel, n, feats), out_shape=(jax.ShapeD...  19.3 us
    unnamed x20, local copies, waits for them, and re-layouts  7.44 us

profile of v3, /device:TPU:1, one launch (start us, length us, event | category | flops | bytes accessed | tf_op | source)
XLA Modules:
  0.0 27.4 jit_solution(2887746183500172208)
XLA Ops:
  0.6 0.0 copy-start.8
  0.6 0.0 copy-start.7
  0.7 0.0 copy-start.6
  0.7 0.6 %copy-done.8 = s32[16]{0:T(128)S(1)} copy-done((s32[16]{0:T(128)S(1)}, s32[16]{0:T(128)}, u32[]{:S(2)}) %copy-start.8) | copy-done | bytes 88
  1.3 0.0 copy-done.7
  1.3 0.0 copy-done.6
  1.3 0.0 copy-start
  1.3 1.1 %copy-done = bf16[128,2560]{1,0:T(8,128)(2,1)S(1)} copy-done((bf16[128,2560]{1,0:T(8,128)(2,1)S(1)}, bf16[128,2560]{1,0:T(8,128)(2,1)}, u32[]{:S(2)}) %copy-start) | copy-done | bytes 655384
  2.4 0.0 copy-start.1
  2.4 1.0 %copy-done.1 = bf16[64,2560]{1,0:T(8,128)(2,1)S(1)} copy-done((bf16[64,2560]{1,0:T(8,128)(2,1)S(1)}, bf16[64,2560]{1,0:T(8,128)(2,1)}, u32[]{:S(2)}) %copy-start.1) | copy-done | bytes 327704
  3.4 0.0 copy-start.2
  3.4 0.9 %copy-done.2 = bf16[128,512]{1,0:T(8,128)(2,1)S(1)} copy-done((bf16[128,512]{1,0:T(8,128)(2,1)S(1)}, bf16[128,512]{1,0:T(8,128)(2,1)}, u32[]{:S(2)}) %copy-start.2) | copy-done | bytes 131096
  4.3 0.0 copy-start.3
  4.3 0.9 %copy-done.3 = bf16[128,512]{1,0:T(8,128)(2,1)S(1)} copy-done((bf16[128,512]{1,0:T(8,128)(2,1)S(1)}, bf16[128,512]{1,0:T(8,128)(2,1)}, u32[]{:S(2)}) %copy-start.3) | copy-done | bytes 131096
  5.2 0.0 copy-start.4
  5.2 0.9 %copy-done.4 = bf16[64,2,512]{2,1,0:T(2,128)(2,1)S(1)} copy-done((bf16[64,2,512]{2,1,0:T(2,128)(2,1)S(1)}, bf16[64,2,512]{2,1,0:T(2,128)(2,1)}, u32[]{:S(2)}) %copy-start.4) | copy-done | bytes 131096
  6.1 0.0 copy-start.5
  6.1 0.7 %copy-done.5 = f32[128,4]{0,1:T(4,128)S(1)} copy-done((f32[128,4]{0,1:T(4,128)S(1)}, f32[128,4]{0,1:T(4,128)}, u32[]{:S(2)}) %copy-start.5) | copy-done | bytes 2072
  6.8 19.3 %shard_map.104 = (bf16[64,2560]{1,0:T(8,128)(2,1)S(1)}, bf16[2,2560]{1,0:T(2,128)(2,1)S(1)}) custom-call(bf16[128,2560]{1,0:T(8,128)(2,1)S(1)} %copy-done, bf16[128,512]{1,0:T(8,128)(2,1)S(1)} %copy-done.2, bf16[128,512]{1,0:T(8,128)(2,1)S(1)} %copy-done.3, f32[4,128]{1,0:T(4,128)S(1)} %bitcast.1, bf16[64,2560]{1,0:T(8,128)(2,1)S(1)} %copy-done.1, ...), custom_call_target="tpu_custom_call" | custom-call | tf_op jit(solution)/shard_map/pallas_call | solution.py:290
  26.1 0.7 %copy.13 = bf16[64,2560]{1,0:T(8,128)(2,1)} copy(bf16[64,2560]{1,0:T(8,128)(2,1)S(1)} %get-tuple-element.4) | data formatting | bytes 655360
  26.8 0.6 %copy.14 = bf16[2,2560]{1,0:T(2,128)(2,1)} copy(bf16[2,2560]{1,0:T(2,128)(2,1)S(1)} %get-tuple-element.5) | data formatting | bytes 20480
Async XLA Ops:
  0.6 0.7 %copy-start.8 = (s32[16]{0:T(128)S(1)}, s32[16]{0:T(128)}, u32[]{:S(2)}) copy-start(s32[16]{0:T(128)} %slot_hbm.1) | copy-start | bytes 196
  0.6 0.7 %copy-start.7 = (s32[16]{0:T(128)S(1)}, s32[16]{0:T(128)}, u32[]{:S(2)}) copy-start(s32[16]{0:T(128)} %fork_hbm.1) | copy-start | bytes 196
  0.7 0.7 %copy-start.6 = (s32[16]{0:T(128)S(1)}, s32[16]{0:T(128)}, u32[]{:S(2)}) copy-start(s32[16]{0:T(128)} %ids_hbm.1) | copy-start | bytes 196
  1.3 1.1 %copy-start = (bf16[128,2560]{1,0:T(8,128)(2,1)S(1)}, bf16[128,2560]{1,0:T(8,128)(2,1)}, u32[]{:S(2)}) copy-start(bf16[128,2560]{1,0:T(8,128)(2,1)} %q_hbm.1) | copy-start | bytes 1966084
  2.4 1.0 %copy-start.1 = (bf16[64,2560]{1,0:T(8,128)(2,1)S(1)}, bf16[64,2560]{1,0:T(8,128)(2,1)}, u32[]{:S(2)}) copy-start(bf16[64,2560]{1,0:T(8,128)(2,1)} %cq_hbm.1) | copy-start | bytes 983044
  3.4 0.9 %copy-start.2 = (bf16[128,512]{1,0:T(8,128)(2,1)S(1)}, bf16[128,512]{1,0:T(8,128)(2,1)}, u32[]{:S(2)}) copy-start(bf16[128,512]{1,0:T(8,128)(2,1)} %k_hbm.1) | copy-start | bytes 393220
  4.3 0.9 %copy-start.3 = (bf16[128,512]{1,0:T(8,128)(2,1)S(1)}, bf16[128,512]{1,0:T(8,128)(2,1)}, u32[]{:S(2)}) copy-start(bf16[128,512]{1,0:T(8,128)(2,1)} %v_hbm.1) | copy-start | bytes 393220
  5.2 0.9 %copy-start.4 = (bf16[64,2,512]{2,1,0:T(2,128)(2,1)S(1)}, bf16[64,2,512]{2,1,0:T(2,128)(2,1)}, u32[]{:S(2)}) copy-start(bf16[64,2,512]{2,1,0:T(2,128)(2,1)} %ckv_hbm.1) | copy-start | bytes 393220
  6.1 0.7 %copy-start.5 = (f32[128,4]{0,1:T(4,128)S(1)}, f32[128,4]{0,1:T(4,128)}, u32[]{:S(2)}) copy-start(f32[128,4]{0,1:T(4,128)} %param.12) | copy-start | bytes 6148

commit v4 on v3

--- a/solution.py
+++ b/solution.py
@@ -314,7 +314,7 @@
             dma((hops * (feats - 1),)), dma((hops * (feats - 1),)),
         ],
         compiler_params=pltpu.CompilerParams(
-            collective_id=0, has_side_effects=True, vmem_limit_bytes=40 * 2**20
+            collective_id=0, has_side_effects=True, vmem_limit_bytes=64 * 2**20 - 2**16
         ),
     )(queries, keys, values, log_gate.T, cand_q, cand_kv, token_ids, fork_pos, slot_map)
 

time: 27.7 us -> 23.2 us (0.84)
  local copies, waits for them, and re-layouts: 7.44 us -> 2.33 us
  Pallas kernels: 19.3 us -> 20.1 us
    unnamed x20 -> x4, local copies, waits for them, and re-layouts: 7.44 us -> 2.33 us
    pallas_call x1, Pallas kernels: 19.3 us -> 20.1 us  [per_device(): pl.pallas_call(functools.partial(kernel, n, feats), out_shape=(jax.ShapeD...]
where the time goes in v4:
time: 23.2 us; the launch traced here: 23.1 us
  Pallas kernels  20.1 us (87%)
  local copies, waits for them, and re-layouts  2.33 us (10%)
  between operations  0.65 us (3%)
    pallas_call x1, Pallas kernels, per_device(): pl.pallas_call(functools.partial(kernel, n, feats), out_shape=(jax.ShapeD...  20.1 us
    unnamed x4, local copies, waits for them, and re-layouts  2.33 us

profile of v4, /device:TPU:1, one launch (start us, length us, event | category | flops | bytes accessed | tf_op | source)
XLA Modules:
  0.0 23.1 jit_solution(15207206931683177669)
XLA Ops:
  0.6 20.1 %shard_map.104 = (bf16[64,2560]{1,0:T(8,128)(2,1)}, bf16[2,2560]{1,0:T(2,128)(2,1)}) custom-call(bf16[128,2560]{1,0:T(8,128)(2,1)} %q_hbm.1, bf16[128,512]{1,0:T(8,128)(2,1)} %k_hbm.1, bf16[128,512]{1,0:T(8,128)(2,1)} %v_hbm.1, f32[4,128]{1,0:T(4,128)} %bitcast.1, bf16[64,2560]{1,0:T(8,128)(2,1)} %cq_hbm.1, bf16[64,2,512]{2,1,0:T(2,128)(2,1)} %ckv_hbm.1, ...), custom_call_target="tpu_custom_call" | custom-call | tf_op jit(solution)/shard_map/pallas_call | solution.py:290
  20.7 0.0 copy-start
  20.7 1.7 %copy.13 = bf16[64,2560]{1,0:T(8,128)(2,1)} copy(bf16[64,2560]{1,0:T(8,128)(2,1)} %get-tuple-element.4) | data formatting | bytes 655360
  22.4 0.0 copy-done
  22.5 0.6 %copy.14 = bf16[2,2560]{1,0:T(2,128)(2,1)} copy(bf16[2,2560]{1,0:T(2,128)(2,1)S(1)} %copy-done) | data formatting | bytes 20480
Async XLA Ops:
  20.7 1.7 %copy-start = (bf16[2,2560]{1,0:T(2,128)(2,1)S(1)}, bf16[2,2560]{1,0:T(2,128)(2,1)}, u32[]{:S(2)}) copy-start(bf16[2,2560]{1,0:T(2,128)(2,1)} %get-tuple-element.5) | copy-start | bytes 30724

commit v5 on v4

--- a/solution.py
+++ b/solution.py
@@ -230,10 +230,10 @@
         add(me, h, True)
 
     for d in range(1, n):
-        for side in range(2):
-            @pl.when(arrives(side, d))
-            def _(side=side, d=d):
-                for part in range(2):
+        for part in range(2):
+            for side in range(2):
+                @pl.when(arrives(side, d))
+                def _(side=side, d=d, part=part):
                     arrival(side, d, part).wait_recv()
                     if d < n - 1:
                         @pl.when(sends(side, d + 1))

time: 23.2 us -> 23.2 us (level)
  no operation moved by 1% of the time
where the time goes in v5:
time: 23.2 us; the launch traced here: 23.1 us
  Pallas kernels  20.1 us (87%)
  local copies, waits for them, and re-layouts  2.33 us (10%)
  between operations  0.65 us (3%)
    pallas_call x1, Pallas kernels, per_device(): pl.pallas_call(functools.partial(kernel, n, feats), out_shape=(jax.ShapeD...  20.1 us
    unnamed x4, local copies, waits for them, and re-layouts  2.33 us

profile of v5, /device:TPU:1, one launch (start us, length us, event | category | flops | bytes accessed | tf_op | source)
XLA Modules:
  0.0 23.1 jit_solution(8404121641214116233)
XLA Ops:
  0.6 20.1 %shard_map.104 = (bf16[64,2560]{1,0:T(8,128)(2,1)}, bf16[2,2560]{1,0:T(2,128)(2,1)}) custom-call(bf16[128,2560]{1,0:T(8,128)(2,1)} %q_hbm.1, bf16[128,512]{1,0:T(8,128)(2,1)} %k_hbm.1, bf16[128,512]{1,0:T(8,128)(2,1)} %v_hbm.1, f32[4,128]{1,0:T(4,128)} %bitcast.1, bf16[64,2560]{1,0:T(8,128)(2,1)} %cq_hbm.1, bf16[64,2,512]{2,1,0:T(2,128)(2,1)} %ckv_hbm.1, ...), custom_call_target="tpu_custom_call" | custom-call | tf_op jit(solution)/shard_map/pallas_call | solution.py:290
  20.7 0.0 copy-start
  20.7 1.7 %copy.13 = bf16[64,2560]{1,0:T(8,128)(2,1)} copy(bf16[64,2560]{1,0:T(8,128)(2,1)} %get-tuple-element.4) | data formatting | bytes 655360
  22.4 0.0 copy-done
  22.5 0.6 %copy.14 = bf16[2,2560]{1,0:T(2,128)(2,1)} copy(bf16[2,2560]{1,0:T(2,128)(2,1)S(1)} %copy-done) | data formatting | bytes 20480
Async XLA Ops:
  20.7 1.7 %copy-start = (bf16[2,2560]{1,0:T(2,128)(2,1)S(1)}, bf16[2,2560]{1,0:T(2,128)(2,1)}, u32[]{:S(2)}) copy-start(bf16[2,2560]{1,0:T(2,128)(2,1)} %get-tuple-element.5) | copy-start | bytes 30724
